TPU v7x, 256 devices: a whole 4x4x8 slice. The times are simulated.
256 devices in a mesh: row: 16 (over x_hi, z), col: 16 (over y, x_lo, core).
Axes of the slice: x: 4 (x_hi: 2, x_lo: 2; x = x_hi * 2 + x_lo), y: 4, z: 8, core: 2. Of those that a mesh axis runs over, the one named last changes fastest.
Arguments:
- streamwise: float32 [384, 256, 1024], P('row', 'col'), may hold values from -6 to 6
- wallnormal: float32 [384, 256, 1024], P('row', 'col'), may hold values from -6 to 6
- spanwise: float32 [384, 256, 1024], P('row', 'col'), may hold values from -6 to 6
- deriv_x: bfloat16 [2, 1024, 1024], replicated, may hold values from -0.1875 to 0.1875
- deriv_y: bfloat16 [2, 384, 384], replicated, may hold values from -0.3125 to 0.3125
- deriv_z: bfloat16 [2, 256, 256], replicated, may hold values from -0.375 to 0.375
Outputs:
- momentum_term: float32 [384, 256, 1024], P('row', 'col')
All inputs are finite; a program needn't handle non-finite values.
Results may differ from a plain program's by a relative error of at most 0.0003.
Values sent between devices are 32-bit elements; how exact they have to be, the bound alone decides.
A program may use at most 128 MiB of HBM per device.

v0:
```python
import functools

import jax
import jax.numpy as jnp
from jax import lax
from jax.experimental import pallas as pl
from jax.experimental.pallas import tpu as pltpu
from jax.sharding import PartitionSpec as P

viscosity = 0.5
MESH = pl.DeviceIdType.MESH
CUTS = 2
ROWS_OF_CUT = 8 // CUTS


def split(value):
    high = value.astype(jnp.bfloat16)
    low = (value - high.astype(jnp.float32)).astype(jnp.bfloat16)
    return high, low


def product(matrix, value):
    high, low = split(value)
    return jnp.dot(matrix, high, preferred_element_type=jnp.float32) + jnp.dot(
        matrix, low, preferred_element_type=jnp.float32
    )


def kernel(
    u_hbm, v_hbm, w_hbm, mx_hbm, my_hbm, mz_hbm, out_hbm,
    u_own, v_own, u_high, mat_x, mat_y, mat_z, u_stage, v_stage,
    u_y, v_y, term_y, back_y, u_z, w_z, term_z, back_z, total,
    load_sem, send_sem, row_sem, col_sem,
):
    row = lax.axis_index("row")
    col = lax.axis_index("col")
    x_low = (col // 2) % 2
    mine = (col // 4) * 2 + col % 2

    def row_peer(shift):
        return lax.rem(row + shift, 16)

    def col_peer(shift):
        other = lax.rem(mine + shift, 8)
        return other, (other // 2) * 4 + x_low * 2 + other % 2

    partner = col + 2 - 4 * x_low

    def lanes_of(x):
        return slice(x * 128, (x + 1) * 128)

    for x in range(8):
        pltpu.make_async_copy(u_hbm.at[:, :, lanes_of(x)], u_own.at[x], load_sem.at[0]).start()
    for x in range(8):
        pltpu.make_async_copy(v_hbm.at[:, :, lanes_of(x)], v_own.at[x], load_sem.at[1]).start()

    barrier = pltpu.get_barrier_semaphore()

    @pl.loop(1, 16)
    def _(shift):
        pl.semaphore_signal(barrier, inc=1, device_id=(row_peer(shift), col), device_id_type=MESH)

    @pl.loop(1, 8)
    def _(shift):
        pl.semaphore_signal(
            barrier, inc=1, device_id=(row, col_peer(shift)[1]), device_id_type=MESH
        )

    pl.semaphore_signal(barrier, inc=1, device_id=(row, partner), device_id_type=MESH)
    pltpu.make_async_copy(mx_hbm, mat_x, load_sem.at[2]).start()
    pltpu.make_async_copy(my_hbm, mat_y, load_sem.at[3]).start()
    pltpu.make_async_copy(mz_hbm, mat_z, load_sem.at[4]).start()

    def restage(own, stage):
        flat = own.reshape(8 * 24 * 16, 128)

        @pl.loop(0, 16)
        def _(z):
            for x in range(8):
                stage[x, z] = flat[pl.ds(x * 384 + z, 24, stride=16), :]

    def send_row(stage, pencil, kind):
        for cut in range(CUTS):
            rows = pl.ds(cut * ROWS_OF_CUT, ROWS_OF_CUT)

            def piece(to):
                return (
                    stage.at[
                        lax.rem(to, 8),
                        pl.ds((to // 8) * 8 + cut * ROWS_OF_CUT, ROWS_OF_CUT),
                    ],
                    pencil.at[rows, pl.ds(pl.multiple_of(row * 24, 8), 24), :],
                )

            def send(shift):
                to = row_peer(shift)
                src, dst = piece(to)
                pltpu.make_async_remote_copy(
                    src_ref=src, dst_ref=dst, send_sem=send_sem.at[kind],
                    recv_sem=row_sem.at[kind, cut], device_id=(to, col), device_id_type=MESH,
                ).start()

            @pl.loop(1, 8)
            def _(shift):
                send(shift)
                send(16 - shift)

            send(8)
            src, dst = piece(row)
            pltpu.make_async_copy(src, dst, row_sem.at[kind, cut]).start()

    def send_col(field, pencil, kind):
        for cut in range(3):

            def piece(to):
                if kind == 0:
                    dst = pencil.at[
                        cut, col // 4, pl.ds(pl.multiple_of((col % 4) * 16, 16), 16), :
                    ]
                else:
                    dst = pencil.at[cut, pl.ds(pl.multiple_of(mine * 16, 16), 16), :]
                return field.at[to * 3 + cut], dst

            @pl.loop(1, 8)
            def _(shift):
                to, to_col = col_peer(shift)
                src, dst = piece(to)
                pltpu.make_async_remote_copy(
                    src_ref=src, dst_ref=dst, send_sem=send_sem.at[3 + kind],
                    recv_sem=col_sem.at[kind, cut], device_id=(row, to_col), device_id_type=MESH,
                ).start()

            src, dst = piece(mine)
            pltpu.make_async_copy(src, dst, col_sem.at[kind, cut]).start()

    def arrived(ref, sem):
        pltpu.make_async_copy(ref, ref, sem).wait()

    arrived(u_own, load_sem.at[0])
    restage(u_own, u_stage)
    pl.semaphore_wait(barrier, 23)
    send_row(u_stage, u_y, 0)
    send_col(u_hbm, u_z, 0)
    arrived(v_own, load_sem.at[1])
    restage(v_own, v_stage)
    send_row(v_stage, v_y, 1)
    send_col(w_hbm, w_z, 1)

    flat_total = total.reshape(8 * 24 * 16, 128)

    for x in range(8):
        high, low = split(u_own[x].reshape(384, 128))
        u_high[:384, lanes_of(x)] = high
        u_high[384:, lanes_of(x)] = low

    arrived(mat_x, load_sem.at[2])

    @pl.loop(0, 4)
    def _(part):
        at = pl.multiple_of(part * 256, 256)

        def along(which):
            both = lax.dot_general(
                u_high[...], mat_x[which, pl.ds(at, 256), :],
                (((1,), (1,)), ((), ())), preferred_element_type=jnp.float32,
            )
            return both[:384] + both[384:]

        first, second = along(0), along(1)
        for i in range(2):
            here = u_own[part * 2 + i].reshape(384, 128)
            term = -here * first[:, lanes_of(i)] + viscosity * second[:, lanes_of(i)]
            total[part * 2 + i] = term.reshape(24, 16, 128)

    arrived(mat_y, load_sem.at[3])
    arrived(mat_z, load_sem.at[4])

    half = pl.ds(pl.multiple_of(x_low * 32, 32), 32)
    other_half = pl.ds(pl.multiple_of(32 - x_low * 32, 32), 32)

    def swap(cut):
        region = u_z.at[cut, :, half, :]
        return pltpu.make_async_remote_copy(
            src_ref=region, dst_ref=region, send_sem=send_sem.at[5],
            recv_sem=col_sem.at[3, cut], device_id=(row, partner), device_id_type=MESH,
        )

    def work_y(cut):
        arrived(u_y.at[pl.ds(cut * ROWS_OF_CUT, ROWS_OF_CUT)], row_sem.at[0, cut])
        arrived(v_y.at[pl.ds(cut * ROWS_OF_CUT, ROWS_OF_CUT)], row_sem.at[1, cut])
        matrix = mat_y[...].reshape(768, 384)

        @pl.loop(0, ROWS_OF_CUT // 2)
        def _(pair):
            z = cut * ROWS_OF_CUT + pair * 2
            both = product(matrix, jnp.concatenate([u_y[z], u_y[z + 1]], axis=1))
            for i in range(2):
                lanes = slice(i * 128, (i + 1) * 128)
                term_y[z + i] = -v_y[z + i] * both[:384, lanes] + viscosity * both[384:, lanes]

        rows = pl.ds(cut * ROWS_OF_CUT, ROWS_OF_CUT)

        def piece(to):
            return (
                term_y.at[rows, pl.ds(pl.multiple_of(to * 24, 8), 24), :],
                back_y.at[
                    lax.rem(row, 8), pl.ds((row // 8) * 8 + cut * ROWS_OF_CUT, ROWS_OF_CUT)
                ],
            )

        def send(shift):
            to = row_peer(shift)
            src, dst = piece(to)
            pltpu.make_async_remote_copy(
                src_ref=src, dst_ref=dst, send_sem=send_sem.at[2],
                recv_sem=row_sem.at[2, cut], device_id=(to, col), device_id_type=MESH,
            ).start()

        @pl.loop(1, 8)
        def _(shift):
            send(shift)
            send(16 - shift)

        send(8)
        src, dst = piece(row)
        pltpu.make_async_copy(src, dst, row_sem.at[2, cut]).start()

    def work_z(cut):
        arrived(u_z.at[cut, :, other_half, :], col_sem.at[3, cut])
        arrived(w_z.at[cut], col_sem.at[1, cut])
        matrix = mat_z[:, :, half, :].reshape(256, 256)
        for tile in range(4):
            lanes = slice(tile * 256, (tile + 1) * 256)
            both = product(matrix, u_z[cut, :, :, lanes].reshape(256, 256))
            term_z[cut, :, lanes] = (
                -w_z[cut, :, lanes] * both[:128] + viscosity * both[128:]
            )

        def piece(to):
            return (
                term_z.at[cut, pl.ds(pl.multiple_of(to * 16, 16), 16), :],
                back_z.at[mine * 3 + cut],
            )

        @pl.loop(1, 8)
        def _(shift):
            to, to_col = col_peer(shift)
            src, dst = piece(to)
            pltpu.make_async_remote_copy(
                src_ref=src, dst_ref=dst, send_sem=send_sem.at[6],
                recv_sem=col_sem.at[2, cut], device_id=(row, to_col), device_id_type=MESH,
            ).start()

        src, dst = piece(mine)
        pltpu.make_async_copy(src, dst, col_sem.at[2, cut]).start()

    for cut in range(3):
        arrived(u_z.at[cut, :, half, :], col_sem.at[0, cut])
        swap(cut).start()
    for cut in range(3):
        work_z(cut)
        if cut < CUTS:
            work_y(cut)
    for cut in range(3, CUTS):
        work_y(cut)

    for cut in range(3):
        arrived(back_z.at[pl.ds(cut * 8, 8)], col_sem.at[2, cut])

    @pl.loop(0, 24)
    def _(y):
        for x in range(8):
            total[x, y] += back_z[y, :, lanes_of(x)]

    for cut in range(CUTS):
        arrived(back_y.at[:, pl.ds(cut * 2 * ROWS_OF_CUT, 2 * ROWS_OF_CUT)], row_sem.at[2, cut])
        for upper in range(2):

            @pl.loop(0, ROWS_OF_CUT)
            def _(step):
                z = upper * 8 + cut * ROWS_OF_CUT + step
                for x in range(8):
                    flat_total[pl.ds(x * 384 + z, 24, stride=16), :] += back_y[x, z]

    for x in range(8):
        pltpu.make_async_copy(total.at[x], out_hbm.at[:, :, lanes_of(x)], load_sem.at[5]).start()

    arrived(u_stage.at[:, pl.ds(0, 15)], send_sem.at[0])
    arrived(v_stage.at[:, pl.ds(0, 15)], send_sem.at[1])
    arrived(back_y.at[:, pl.ds(0, 15)], send_sem.at[2])
    arrived(back_z.at[pl.ds(0, 21)], send_sem.at[3])
    arrived(back_z.at[pl.ds(0, 21)], send_sem.at[4])
    arrived(back_z, send_sem.at[5])
    arrived(back_z.at[pl.ds(0, 21)], send_sem.at[6])
    arrived(total, load_sem.at[5])


def shards(u, v, w, deriv_x, deriv_y, deriv_z):
    f32, bf16 = jnp.float32, jnp.bfloat16
    field = pltpu.VMEM((24, 16, 1024), f32)
    tiled = pltpu.VMEM((8, 24, 16, 128), f32)
    staged = pltpu.VMEM((8, 16, 24, 128), f32)
    pencil_y = pltpu.VMEM((8, 384, 128), f32)
    half_z = pltpu.VMEM((3, 128, 1024), f32)
    return pl.pallas_call(
        kernel,
        out_shape=jax.ShapeDtypeStruct((24, 16, 1024), f32),
        in_specs=[pl.BlockSpec(memory_space=pl.ANY)] * 6,
        out_specs=pl.BlockSpec(memory_space=pl.ANY),
        scratch_shapes=[
            tiled, tiled, pltpu.VMEM((768, 1024), bf16),
            pltpu.VMEM((2, 1024, 1024), bf16), pltpu.VMEM((2, 384, 384), bf16),
            pltpu.VMEM((2, 4, 64, 256), bf16),
            staged, staged, pencil_y, pencil_y, pencil_y, staged,
            pltpu.VMEM((3, 4, 64, 1024), f32), half_z, half_z, field, tiled,
            pltpu.SemaphoreType.DMA((6,)), pltpu.SemaphoreType.DMA((7,)),
            pltpu.SemaphoreType.DMA((3, CUTS)), pltpu.SemaphoreType.DMA((4, 3)),
        ],
        compiler_params=pltpu.CompilerParams(
            collective_id=0, has_side_effects=True, vmem_limit_bytes=52 * 2**20
        ),
        cost_estimate=pl.CostEstimate(flops=5 * 10**9, bytes_accessed=12 * 2**20, transcendentals=0),
        name="momentum",
    )(u, v, w, deriv_x, deriv_y, deriv_z.reshape(2, 4, 64, 256))


def solution(mesh):
    placed = (P("row", "col", None), P("row", "col", None), P("row", "col", None), P(), P(), P())
    return jax.shard_map(
        shards, mesh=mesh, in_specs=placed, out_specs=P("row", "col", None), check_vma=False
    )
```

profile of v0, /device:TPU:1, one launch (start us, length us, event | category | flops | bytes accessed | tf_op | source)
XLA Modules:
  0.0 118.9 jit_solution(13409708841007434147)
XLA Ops:
  0.0 0.0 copy-start
  0.0 1.1 copy-done
  1.1 0.0 copy-start.1
  1.1 0.9 copy-done.1
  2.0 114.1 %momentum.1 = f32[24,16,1024]{2,1,0:T(8,128)} custom-call(f32[24,16,1024]{2,1,0:T(8,128)} %u_hbm.1, f32[24,16,1024]{2,1,0:T(8,128)} %v_hbm.1, f32[24,16,1024]{2,1,0:T(8,128)} %w_hbm.1, bf16[2,1024,1024]{2,1,0:T(8,128)(2,1)} %mx_hbm.1, bf16[2,384,384]{2,1,0:T(8,128)(2,1)S(1)} %copy-done, bf16[2,4,64,256]{3,2,1,0:T(8,128)(2,1)S(1)} %bitcast.1), custom_call_target="tpu_custom_call" | custom-call | flops 5000000000 | bytes 12582912 | tf_op jit(solution)/shard_map/momentum/pallas_call | solution.py:305
  116.2 2.7 %copy.8 = f32[24,16,1024]{2,1,0:T(8,128)} copy(f32[24,16,1024]{2,1,0:T(8,128)} %momentum.1) | data formatting | bytes 3145728
Async XLA Ops:
  0.0 1.1 copy-start
  1.1 0.9 copy-start.1
where the time goes:
time: 119 us
  Pallas kernels  114 us (96%)
  local copies, waits for them, and re-layouts  4.74 us (4%)
    pallas_call x1, Pallas kernels, shards(): pl.pallas_call(kernel, out_shape=jax.ShapeDtypeStruct((24, 16, 1024), f32...  114 us
    unnamed x5, local copies, waits for them, and re-layouts  4.74 us

commit v1 on v0

--- a/solution.py
+++ b/solution.py
@@ -27,9 +27,9 @@
 
 
 def kernel(
-    u_hbm, v_hbm, w_hbm, mx_hbm, my_hbm, mz_hbm, out_hbm,
-    u_own, v_own, u_high, mat_x, mat_y, mat_z, u_stage, v_stage,
-    u_y, v_y, term_y, back_y, u_z, w_z, term_z, back_z, total,
+    u_hbm, v_hbm, w_hbm, mx_hbm, my_hbm, mz_hbm, total,
+    u_own, v_own, u_high, mat_x, mat_y, mat_z, rows_y, lhs_y, u_stage, v_stage,
+    u_y, v_y, term_y, back_y, u_z, w_z, term_z, back_z,
     load_sem, send_sem, row_sem, col_sem,
 ):
     row = lax.axis_index("row")
@@ -37,8 +37,13 @@
     x_low = (col // 2) % 2
     mine = (col // 4) * 2 + col % 2
 
-    def row_peer(shift):
-        return lax.rem(row + shift, 16)
+    x_me, z_me = row // 8, lax.rem(row, 8)
+
+    def around(z):
+        return lax.rem(z + 8, 8)
+
+    def row_of(x, z):
+        return x * 8 + around(z)
 
     def col_peer(shift):
         other = lax.rem(mine + shift, 8)
@@ -56,9 +61,16 @@
 
     barrier = pltpu.get_barrier_semaphore()
 
-    @pl.loop(1, 16)
-    def _(shift):
-        pl.semaphore_signal(barrier, inc=1, device_id=(row_peer(shift), col), device_id_type=MESH)
+    def greet(x, z):
+        pl.semaphore_signal(barrier, inc=1, device_id=(row_of(x, z), col), device_id_type=MESH)
+
+    @pl.loop(1, 4)
+    def _(j):
+        for z in (z_me + j, z_me - j):
+            greet(x_me, z)
+            greet(1 - x_me, z)
+
+    greet(1 - x_me, z_me)
 
     @pl.loop(1, 8)
     def _(shift):
@@ -71,43 +83,65 @@
     pltpu.make_async_copy(my_hbm, mat_y, load_sem.at[3]).start()
     pltpu.make_async_copy(mz_hbm, mat_z, load_sem.at[4]).start()
 
-    def restage(own, stage):
+    def restage(own, stage, cut):
         flat = own.reshape(8 * 24 * 16, 128)
-
-        @pl.loop(0, 16)
-        def _(z):
-            for x in range(8):
-                stage[x, z] = flat[pl.ds(x * 384 + z, 24, stride=16), :]
-
-    def send_row(stage, pencil, kind):
-        for cut in range(CUTS):
+        for upper in range(2):
+
+            @pl.loop(0, ROWS_OF_CUT)
+            def _(step):
+                z = upper * 8 + cut * ROWS_OF_CUT + step
+                for x in range(8):
+                    stage[x, z] = flat[pl.ds(x * 384 + z, 24, stride=16), :]
+
+    def over_row(piece, kind, cut, sems):
+        def send(x, j, role):
+            src, dst, to = piece(x, j, role)
+            pltpu.make_async_remote_copy(
+                src_ref=src, dst_ref=dst, send_sem=send_sem.at[kind],
+                recv_sem=sems(role), device_id=(to, col), device_id_type=MESH,
+            ).start()
+
+        @pl.loop(0, 3)
+        def _(step):
+            for role in range(2):
+                send(1 - x_me, 3 - step, role)
+                send(x_me, 3 - step, role)
+
+        for role in range(2):
+            send(1 - x_me, 0, role)
+            src, dst, _ = piece(x_me, 0, role)
+            pltpu.make_async_copy(src, dst, sems(role)).start()
+
+    def send_row(stage, pencil, kind, cut):
+        rows = pl.ds(cut * ROWS_OF_CUT, ROWS_OF_CUT)
+
+        def piece(x, j, role):
+            to = around(z_me + j) if role == 0 else around(z_me - j)
+            group = to if role == 0 else around(to - 1)
+            src = stage.at[group, pl.ds(x * 8 + cut * ROWS_OF_CUT, ROWS_OF_CUT)]
+            if kind == 0:
+                dst = pencil.at[role, rows, x_me, pl.ds(pl.multiple_of(z_me * 24, 8), 24), :]
+            else:
+                slot = x_me * 4 + (3 - j if role == 0 else j)
+                dst = pencil.at[role, rows, pl.ds(pl.multiple_of(slot * 24, 8), 24), :]
+            return src, dst, x * 8 + to
+
+        over_row(piece, kind, cut, lambda role: row_sem.at[kind * 2 + role, cut])
+
+    def exchange(role, cut):
+        to = row_of(x_me, z_me + 1 - 2 * role)
+
+        @pl.loop(0, 4)
+        def _(i):
+            z = around(z_me - 3 + i + 3 * role)
+            at = pl.ds(pl.multiple_of(z * 24, 8), 24)
             rows = pl.ds(cut * ROWS_OF_CUT, ROWS_OF_CUT)
-
-            def piece(to):
-                return (
-                    stage.at[
-                        lax.rem(to, 8),
-                        pl.ds((to // 8) * 8 + cut * ROWS_OF_CUT, ROWS_OF_CUT),
-                    ],
-                    pencil.at[rows, pl.ds(pl.multiple_of(row * 24, 8), 24), :],
-                )
-
-            def send(shift):
-                to = row_peer(shift)
-                src, dst = piece(to)
-                pltpu.make_async_remote_copy(
-                    src_ref=src, dst_ref=dst, send_sem=send_sem.at[kind],
-                    recv_sem=row_sem.at[kind, cut], device_id=(to, col), device_id_type=MESH,
-                ).start()
-
-            @pl.loop(1, 8)
-            def _(shift):
-                send(shift)
-                send(16 - shift)
-
-            send(8)
-            src, dst = piece(row)
-            pltpu.make_async_copy(src, dst, row_sem.at[kind, cut]).start()
+            pltpu.make_async_remote_copy(
+                src_ref=u_y.at[role, rows, :, at, :],
+                dst_ref=u_y.at[1 - role, rows, :, at, :],
+                send_sem=send_sem.at[7], recv_sem=row_sem.at[5 + 1 - role, cut],
+                device_id=(to, col), device_id_type=MESH,
+            ).start()
 
     def send_col(field, pencil, kind):
         for cut in range(3):
@@ -137,13 +171,17 @@
         pltpu.make_async_copy(ref, ref, sem).wait()
 
     arrived(u_own, load_sem.at[0])
-    restage(u_own, u_stage)
-    pl.semaphore_wait(barrier, 23)
-    send_row(u_stage, u_y, 0)
+    restage(u_own, u_stage, 0)
+    pl.semaphore_wait(barrier, 21)
+    send_row(u_stage, u_y, 0, 0)
     send_col(u_hbm, u_z, 0)
+    for cut in range(1, CUTS):
+        restage(u_own, u_stage, cut)
+        send_row(u_stage, u_y, 0, cut)
     arrived(v_own, load_sem.at[1])
-    restage(v_own, v_stage)
-    send_row(v_stage, v_y, 1)
+    for cut in range(CUTS):
+        restage(v_own, v_stage, cut)
+        send_row(v_stage, v_y, 1, cut)
     send_col(w_hbm, w_z, 1)
 
     flat_total = total.reshape(8 * 24 * 16, 128)
@@ -174,6 +212,21 @@
 
     arrived(mat_y, load_sem.at[3])
     arrived(mat_z, load_sem.at[4])
+
+    rows_y[...] = mat_y[...].astype(jnp.float32)
+    for role in range(2):
+        for which in range(2):
+            for x in range(2):
+                for pair in range(2):
+                    some = []
+                    for j in (2 * pair, 2 * pair + 1):
+                        z = around(z_me - 3 + j + 3 * role)
+                        at = pl.multiple_of(x * 192 + z * 24, 8)
+                        some.append(rows_y[which, pl.ds(at, 24), :])
+                    start = which * 192 + x * 96 + pair * 48
+                    lhs_y[role, start : start + 48, :] = jnp.concatenate(some, axis=0).astype(
+                        jnp.bfloat16
+                    )
 
     half = pl.ds(pl.multiple_of(x_low * 32, 32), 32)
     other_half = pl.ds(pl.multiple_of(32 - x_low * 32, 32), 32)
@@ -185,45 +238,44 @@
             recv_sem=col_sem.at[3, cut], device_id=(row, partner), device_id_type=MESH,
         )
 
-    def work_y(cut):
-        arrived(u_y.at[pl.ds(cut * ROWS_OF_CUT, ROWS_OF_CUT)], row_sem.at[0, cut])
-        arrived(v_y.at[pl.ds(cut * ROWS_OF_CUT, ROWS_OF_CUT)], row_sem.at[1, cut])
-        matrix = mat_y[...].reshape(768, 384)
+    def own_half(role, cut):
+        arrived(v_y.at[role, pl.ds(cut * ROWS_OF_CUT, ROWS_OF_CUT)], row_sem.at[role, cut])
+
+    def work_y(role, cut):
+        rows = pl.ds(cut * ROWS_OF_CUT, ROWS_OF_CUT)
+        arrived(v_y.at[role, rows], row_sem.at[5 + role, cut])
+        arrived(v_y.at[role, rows], row_sem.at[2 + role, cut])
 
         @pl.loop(0, ROWS_OF_CUT // 2)
         def _(pair):
             z = cut * ROWS_OF_CUT + pair * 2
-            both = product(matrix, jnp.concatenate([u_y[z], u_y[z + 1]], axis=1))
+            both = product(
+                lhs_y[role],
+                jnp.concatenate(
+                    [u_y[role, z + i].reshape(384, 128) for i in range(2)], axis=1
+                ),
+            )
             for i in range(2):
-                lanes = slice(i * 128, (i + 1) * 128)
-                term_y[z + i] = -v_y[z + i] * both[:384, lanes] + viscosity * both[384:, lanes]
-
+                lanes = lanes_of(i)
+                term_y[role, z + i] = (
+                    -v_y[role, z + i] * both[:192, lanes] + viscosity * both[192:, lanes]
+                )
+
+    def return_y(cut):
         rows = pl.ds(cut * ROWS_OF_CUT, ROWS_OF_CUT)
 
-        def piece(to):
+        def piece(x, j, role):
+            to = around(z_me - j) if role == 0 else around(z_me + j)
+            slot = x * 4 + (3 - j if role == 0 else j)
             return (
-                term_y.at[rows, pl.ds(pl.multiple_of(to * 24, 8), 24), :],
+                term_y.at[role, rows, pl.ds(pl.multiple_of(slot * 24, 8), 24), :],
                 back_y.at[
-                    lax.rem(row, 8), pl.ds((row // 8) * 8 + cut * ROWS_OF_CUT, ROWS_OF_CUT)
+                    around(z_me - role), pl.ds(x_me * 8 + cut * ROWS_OF_CUT, ROWS_OF_CUT)
                 ],
-            )
-
-        def send(shift):
-            to = row_peer(shift)
-            src, dst = piece(to)
-            pltpu.make_async_remote_copy(
-                src_ref=src, dst_ref=dst, send_sem=send_sem.at[2],
-                recv_sem=row_sem.at[2, cut], device_id=(to, col), device_id_type=MESH,
-            ).start()
-
-        @pl.loop(1, 8)
-        def _(shift):
-            send(shift)
-            send(16 - shift)
-
-        send(8)
-        src, dst = piece(row)
-        pltpu.make_async_copy(src, dst, row_sem.at[2, cut]).start()
+                x * 8 + to,
+            )
+
+        over_row(piece, 2, cut, lambda role: row_sem.at[4, cut])
 
     def work_z(cut):
         arrived(u_z.at[cut, :, other_half, :], col_sem.at[3, cut])
@@ -257,12 +309,17 @@
     for cut in range(3):
         arrived(u_z.at[cut, :, half, :], col_sem.at[0, cut])
         swap(cut).start()
-    for cut in range(3):
-        work_z(cut)
+    for cut in range(CUTS):
+        for role in range(2):
+            own_half(role, cut)
+            exchange(role, cut)
+    for cut in range(max(3, CUTS)):
+        if cut < 3:
+            work_z(cut)
         if cut < CUTS:
-            work_y(cut)
-    for cut in range(3, CUTS):
-        work_y(cut)
+            work_y(0, cut)
+            work_y(1, cut)
+            return_y(cut)
 
     for cut in range(3):
         arrived(back_z.at[pl.ds(cut * 8, 8)], col_sem.at[2, cut])
@@ -273,7 +330,7 @@
             total[x, y] += back_z[y, :, lanes_of(x)]
 
     for cut in range(CUTS):
-        arrived(back_y.at[:, pl.ds(cut * 2 * ROWS_OF_CUT, 2 * ROWS_OF_CUT)], row_sem.at[2, cut])
+        arrived(back_y.at[:, pl.ds(cut * 2 * ROWS_OF_CUT, 2 * ROWS_OF_CUT)], row_sem.at[4, cut])
         for upper in range(2):
 
             @pl.loop(0, ROWS_OF_CUT)
@@ -282,17 +339,14 @@
                 for x in range(8):
                     flat_total[pl.ds(x * 384 + z, 24, stride=16), :] += back_y[x, z]
 
-    for x in range(8):
-        pltpu.make_async_copy(total.at[x], out_hbm.at[:, :, lanes_of(x)], load_sem.at[5]).start()
-
-    arrived(u_stage.at[:, pl.ds(0, 15)], send_sem.at[0])
-    arrived(v_stage.at[:, pl.ds(0, 15)], send_sem.at[1])
-    arrived(back_y.at[:, pl.ds(0, 15)], send_sem.at[2])
+    arrived(u_stage.at[:, pl.ds(0, 14)], send_sem.at[0])
+    arrived(v_stage.at[:, pl.ds(0, 14)], send_sem.at[1])
+    arrived(back_y.at[:, pl.ds(0, 14)], send_sem.at[2])
+    arrived(back_y, send_sem.at[7])
     arrived(back_z.at[pl.ds(0, 21)], send_sem.at[3])
     arrived(back_z.at[pl.ds(0, 21)], send_sem.at[4])
     arrived(back_z, send_sem.at[5])
     arrived(back_z.at[pl.ds(0, 21)], send_sem.at[6])
-    arrived(total, load_sem.at[5])
 
 
 def shards(u, v, w, deriv_x, deriv_y, deriv_z):
@@ -300,28 +354,30 @@
     field = pltpu.VMEM((24, 16, 1024), f32)
     tiled = pltpu.VMEM((8, 24, 16, 128), f32)
     staged = pltpu.VMEM((8, 16, 24, 128), f32)
-    pencil_y = pltpu.VMEM((8, 384, 128), f32)
+    half_y = pltpu.VMEM((2, 8, 192, 128), f32)
     half_z = pltpu.VMEM((3, 128, 1024), f32)
-    return pl.pallas_call(
+    result = pl.pallas_call(
         kernel,
-        out_shape=jax.ShapeDtypeStruct((24, 16, 1024), f32),
+        out_shape=pltpu.VMEM((8, 24, 16, 128), f32),
         in_specs=[pl.BlockSpec(memory_space=pl.ANY)] * 6,
-        out_specs=pl.BlockSpec(memory_space=pl.ANY),
+        out_specs=pl.BlockSpec(memory_space=pltpu.VMEM),
         scratch_shapes=[
             tiled, tiled, pltpu.VMEM((768, 1024), bf16),
             pltpu.VMEM((2, 1024, 1024), bf16), pltpu.VMEM((2, 384, 384), bf16),
             pltpu.VMEM((2, 4, 64, 256), bf16),
-            staged, staged, pencil_y, pencil_y, pencil_y, staged,
-            pltpu.VMEM((3, 4, 64, 1024), f32), half_z, half_z, field, tiled,
-            pltpu.SemaphoreType.DMA((6,)), pltpu.SemaphoreType.DMA((7,)),
-            pltpu.SemaphoreType.DMA((3, CUTS)), pltpu.SemaphoreType.DMA((4, 3)),
+            pltpu.VMEM((2, 384, 384), f32), pltpu.VMEM((2, 384, 384), bf16),
+            staged, staged, pltpu.VMEM((2, 8, 2, 192, 128), f32), half_y, half_y, staged,
+            pltpu.VMEM((3, 4, 64, 1024), f32), half_z, half_z, field,
+            pltpu.SemaphoreType.DMA((5,)), pltpu.SemaphoreType.DMA((8,)),
+            pltpu.SemaphoreType.DMA((7, CUTS)), pltpu.SemaphoreType.DMA((4, 3)),
         ],
         compiler_params=pltpu.CompilerParams(
-            collective_id=0, has_side_effects=True, vmem_limit_bytes=52 * 2**20
+            collective_id=0, has_side_effects=True, vmem_limit_bytes=60 * 2**20
         ),
         cost_estimate=pl.CostEstimate(flops=5 * 10**9, bytes_accessed=12 * 2**20, transcendentals=0),
         name="momentum",
     )(u, v, w, deriv_x, deriv_y, deriv_z.reshape(2, 4, 64, 256))
+    return jnp.transpose(result, (1, 2, 0, 3)).reshape(24, 16, 1024)
 
 
 def solution(mesh):

time: 119 us -> 107 us (0.90)
  Pallas kernels: 114 us -> 106 us
  local copies, waits for them, and re-layouts: 4.74 us -> 1.35 us
    pallas_call x1, Pallas kernels: 114 us -> 106 us  [shards(): pl.pallas_call(kernel, out_shape=pltpu.VMEM((8, 24, 16, 128), f32), in_sp...]
    unnamed x5 -> x0, local copies, waits for them, and re-layouts: 4.74 us -> none
    reshape x0 -> x1, local copies, waits for them, and re-layouts: none -> 1.35 us  [shards(): return jnp.transpose(result, (1, 2, 0, 3)).reshape(24, 16, 1024)]
where the time goes in v1:
time: 107 us
  Pallas kernels  106 us (99%)
  local copies, waits for them, and re-layouts  1.35 us (1%)
    pallas_call x1, Pallas kernels, shards(): pl.pallas_call(kernel, out_shape=pltpu.VMEM((8, 24, 16, 128), f32), in_sp...  106 us

profile of v1, /device:TPU:1, one launch (start us, length us, event | category | flops | bytes accessed | tf_op | source)
XLA Modules:
  0.0 107.1 jit_solution(2496742237144048616)
XLA Ops:
  0.0 105.8 %momentum.1 = f32[8,24,16,128]{3,2,1,0:T(8,128)S(1)} custom-call(f32[24,16,1024]{2,1,0:T(8,128)} %u_hbm.1, f32[24,16,1024]{2,1,0:T(8,128)} %v_hbm.1, f32[24,16,1024]{2,1,0:T(8,128)} %w_hbm.1, bf16[2,1024,1024]{2,1,0:T(8,128)(2,1)} %mx_hbm.1, bf16[2,384,384]{2,1,0:T(8,128)(2,1)} %my_hbm.1, bf16[2,4,64,256]{3,2,1,0:T(8,128)(2,1)} %bitcast.7), custom_call_target="tpu_custom_call" | custom-call | flops 5000000000 | bytes 12582912 | tf_op jit(solution)/shard_map/momentum/pallas_call | solution.py:359
  105.8 1.3 %copy_bitcast_fusion = f32[24,16,1024]{2,1,0:T(8,128)} fusion(f32[8,24,16,128]{3,2,1,0:T(8,128)S(1)} %momentum.1), kind=kLoop, calls=%fused_computation | loop fusion | bytes 3145728 | tf_op jit(solution)/shard_map/reshape | solution.py:380

commit v2 on v1

--- a/solution.py
+++ b/solution.py
@@ -9,8 +9,11 @@
 
 viscosity = 0.5
 MESH = pl.DeviceIdType.MESH
-CUTS = 2
+CUTS = 4
 ROWS_OF_CUT = 8 // CUTS
+BASE = (0, 288, 336, 144)
+SERVED = (144, 48, 48, 144)
+ROUTES = ((0, 2), (3, 2), (0, 1), (3, 1), (0, 0), (3, 0), (1, 0), (2, 0))
 
 
 def split(value):
@@ -64,12 +67,9 @@
     def greet(x, z):
         pl.semaphore_signal(barrier, inc=1, device_id=(row_of(x, z), col), device_id_type=MESH)
 
-    @pl.loop(1, 4)
-    def _(j):
-        for z in (z_me + j, z_me - j):
-            greet(x_me, z)
-            greet(1 - x_me, z)
-
+    for z in (z_me - 2, z_me - 1, z_me + 1, z_me + 2):
+        greet(x_me, z)
+        greet(1 - x_me, z)
     greet(1 - x_me, z_me)
 
     @pl.loop(1, 8)
@@ -83,6 +83,9 @@
     pltpu.make_async_copy(my_hbm, mat_y, load_sem.at[3]).start()
     pltpu.make_async_copy(mz_hbm, mat_z, load_sem.at[4]).start()
 
+    def arrived(ref, sem):
+        pltpu.make_async_copy(ref, ref, sem).wait()
+
     def restage(own, stage, cut):
         flat = own.reshape(8 * 24 * 16, 128)
         for upper in range(2):
@@ -93,55 +96,69 @@
                 for x in range(8):
                     stage[x, z] = flat[pl.ds(x * 384 + z, 24, stride=16), :]
 
+    def slot(role, j, x):
+        served = 2 - j if role == 0 else j
+        return pl.ds(pl.multiple_of(BASE[role] + served * 48 + x * 24, 8), 24)
+
     def over_row(piece, kind, cut, sems):
-        def send(x, j, role):
-            src, dst, to = piece(x, j, role)
-            pltpu.make_async_remote_copy(
-                src_ref=src, dst_ref=dst, send_sem=send_sem.at[kind],
-                recv_sem=sems(role), device_id=(to, col), device_id_type=MESH,
-            ).start()
-
-        @pl.loop(0, 3)
-        def _(step):
-            for role in range(2):
-                send(1 - x_me, 3 - step, role)
-                send(x_me, 3 - step, role)
-
-        for role in range(2):
-            send(1 - x_me, 0, role)
-            src, dst, _ = piece(x_me, 0, role)
-            pltpu.make_async_copy(src, dst, sems(role)).start()
+        for role, j in ROUTES:
+            for x in (1 - x_me, x_me):
+                src, dst, to = piece(x, j, role)
+                if j == 0 and x is x_me:
+                    pltpu.make_async_copy(src, dst, sems(role)).start()
+                else:
+                    pltpu.make_async_remote_copy(
+                        src_ref=src, dst_ref=dst, send_sem=send_sem.at[kind],
+                        recv_sem=sems(role), device_id=(to, col), device_id_type=MESH,
+                    ).start()
 
     def send_row(stage, pencil, kind, cut):
         rows = pl.ds(cut * ROWS_OF_CUT, ROWS_OF_CUT)
 
         def piece(x, j, role):
             to = around(z_me + j) if role == 0 else around(z_me - j)
-            group = to if role == 0 else around(to - 1)
+            group = around(to - role)
             src = stage.at[group, pl.ds(x * 8 + cut * ROWS_OF_CUT, ROWS_OF_CUT)]
             if kind == 0:
                 dst = pencil.at[role, rows, x_me, pl.ds(pl.multiple_of(z_me * 24, 8), 24), :]
             else:
-                slot = x_me * 4 + (3 - j if role == 0 else j)
-                dst = pencil.at[role, rows, pl.ds(pl.multiple_of(slot * 24, 8), 24), :]
+                dst = pencil.at[rows, slot(role, j, x_me), :]
             return src, dst, x * 8 + to
 
-        over_row(piece, kind, cut, lambda role: row_sem.at[kind * 2 + role, cut])
-
-    def exchange(role, cut):
-        to = row_of(x_me, z_me + 1 - 2 * role)
-
-        @pl.loop(0, 4)
+        over_row(
+            piece, kind, cut,
+            lambda role: row_sem.at[role, cut] if kind == 0 else row_sem.at[4, cut],
+        )
+
+    def pass_on(role, step, cut):
+        to = row_of(x_me, z_me + step)
+        first = z_me - role - 2 if step == 1 else z_me
+        rows = pl.ds(cut * ROWS_OF_CUT, ROWS_OF_CUT)
+
+        @pl.loop(0, 3 + role if step == 1 else 6 - role)
         def _(i):
-            z = around(z_me - 3 + i + 3 * role)
+            z = around(first + i)
             at = pl.ds(pl.multiple_of(z * 24, 8), 24)
-            rows = pl.ds(cut * ROWS_OF_CUT, ROWS_OF_CUT)
             pltpu.make_async_remote_copy(
                 src_ref=u_y.at[role, rows, :, at, :],
-                dst_ref=u_y.at[1 - role, rows, :, at, :],
-                send_sem=send_sem.at[7], recv_sem=row_sem.at[5 + 1 - role, cut],
+                dst_ref=u_y.at[role + step, rows, :, at, :],
+                send_sem=send_sem.at[7],
+                recv_sem=row_sem.at[(5 if step == 1 else 9) + role + step, cut],
                 device_id=(to, col), device_id_type=MESH,
             ).start()
+
+    def came_in(role, step, cut):
+        count = 2 + role if step == 1 else 5 - role
+        arrived(
+            v_y.at[pl.ds(cut * ROWS_OF_CUT, ROWS_OF_CUT), pl.ds(0, 48 * count)],
+            row_sem.at[(5 if step == 1 else 9) + role, cut],
+        )
+
+    def own_part(role, cut):
+        arrived(
+            v_y.at[pl.ds(cut * ROWS_OF_CUT, ROWS_OF_CUT), pl.ds(BASE[role], SERVED[role])],
+            row_sem.at[role, cut],
+        )
 
     def send_col(field, pencil, kind):
         for cut in range(3):
@@ -167,12 +184,9 @@
             src, dst = piece(mine)
             pltpu.make_async_copy(src, dst, col_sem.at[kind, cut]).start()
 
-    def arrived(ref, sem):
-        pltpu.make_async_copy(ref, ref, sem).wait()
-
     arrived(u_own, load_sem.at[0])
     restage(u_own, u_stage, 0)
-    pl.semaphore_wait(barrier, 21)
+    pl.semaphore_wait(barrier, 17)
     send_row(u_stage, u_y, 0, 0)
     send_col(u_hbm, u_z, 0)
     for cut in range(1, CUTS):
@@ -214,19 +228,18 @@
     arrived(mat_z, load_sem.at[4])
 
     rows_y[...] = mat_y[...].astype(jnp.float32)
-    for role in range(2):
+    for role in range(4):
         for which in range(2):
-            for x in range(2):
-                for pair in range(2):
-                    some = []
-                    for j in (2 * pair, 2 * pair + 1):
-                        z = around(z_me - 3 + j + 3 * role)
-                        at = pl.multiple_of(x * 192 + z * 24, 8)
-                        some.append(rows_y[which, pl.ds(at, 24), :])
-                    start = which * 192 + x * 96 + pair * 48
-                    lhs_y[role, start : start + 48, :] = jnp.concatenate(some, axis=0).astype(
-                        jnp.bfloat16
-                    )
+            for served in range(SERVED[role] // 48):
+                z = around(z_me + (served - 2 if role == 0 else served))
+                both_x = [
+                    rows_y[which, pl.ds(pl.multiple_of(x * 192 + z * 24, 8), 24), :]
+                    for x in range(2)
+                ]
+                start = 2 * BASE[role] + which * SERVED[role] + served * 48
+                lhs_y[start : start + 48, :] = jnp.concatenate(both_x, axis=0).astype(
+                    jnp.bfloat16
+                )
 
     half = pl.ds(pl.multiple_of(x_low * 32, 32), 32)
     other_half = pl.ds(pl.multiple_of(32 - x_low * 32, 32), 32)
@@ -238,27 +251,23 @@
             recv_sem=col_sem.at[3, cut], device_id=(row, partner), device_id_type=MESH,
         )
 
-    def own_half(role, cut):
-        arrived(v_y.at[role, pl.ds(cut * ROWS_OF_CUT, ROWS_OF_CUT)], row_sem.at[role, cut])
-
     def work_y(role, cut):
-        rows = pl.ds(cut * ROWS_OF_CUT, ROWS_OF_CUT)
-        arrived(v_y.at[role, rows], row_sem.at[5 + role, cut])
-        arrived(v_y.at[role, rows], row_sem.at[2 + role, cut])
+        base, count = BASE[role], SERVED[role]
 
         @pl.loop(0, ROWS_OF_CUT // 2)
         def _(pair):
             z = cut * ROWS_OF_CUT + pair * 2
             both = product(
-                lhs_y[role],
+                lhs_y[2 * base : 2 * (base + count), :],
                 jnp.concatenate(
                     [u_y[role, z + i].reshape(384, 128) for i in range(2)], axis=1
                 ),
             )
             for i in range(2):
                 lanes = lanes_of(i)
-                term_y[role, z + i] = (
-                    -v_y[role, z + i] * both[:192, lanes] + viscosity * both[192:, lanes]
+                term_y[z + i, base : base + count] = (
+                    -v_y[z + i, base : base + count] * both[:count, lanes]
+                    + viscosity * both[count:, lanes]
                 )
 
     def return_y(cut):
@@ -266,16 +275,15 @@
 
         def piece(x, j, role):
             to = around(z_me - j) if role == 0 else around(z_me + j)
-            slot = x * 4 + (3 - j if role == 0 else j)
             return (
-                term_y.at[role, rows, pl.ds(pl.multiple_of(slot * 24, 8), 24), :],
+                term_y.at[rows, slot(role, j, x), :],
                 back_y.at[
                     around(z_me - role), pl.ds(x_me * 8 + cut * ROWS_OF_CUT, ROWS_OF_CUT)
                 ],
                 x * 8 + to,
             )
 
-        over_row(piece, 2, cut, lambda role: row_sem.at[4, cut])
+        over_row(piece, 2, cut, lambda role: row_sem.at[5, cut])
 
     def work_z(cut):
         arrived(u_z.at[cut, :, other_half, :], col_sem.at[3, cut])
@@ -306,19 +314,37 @@
         src, dst = piece(mine)
         pltpu.make_async_copy(src, dst, col_sem.at[2, cut]).start()
 
+    for cut in range(CUTS):
+        own_part(0, cut)
+        pass_on(0, 1, cut)
+        own_part(3, cut)
+        pass_on(3, -1, cut)
     for cut in range(3):
         arrived(u_z.at[cut, :, half, :], col_sem.at[0, cut])
         swap(cut).start()
     for cut in range(CUTS):
-        for role in range(2):
-            own_half(role, cut)
-            exchange(role, cut)
+        came_in(1, 1, cut)
+        own_part(1, cut)
+        pass_on(1, 1, cut)
+        came_in(2, -1, cut)
+        own_part(2, cut)
+        pass_on(2, -1, cut)
+    for cut in range(CUTS):
+        came_in(2, 1, cut)
+        pass_on(2, 1, cut)
+        came_in(1, -1, cut)
+        pass_on(1, -1, cut)
     for cut in range(max(3, CUTS)):
         if cut < 3:
             work_z(cut)
         if cut < CUTS:
+            arrived(v_y.at[pl.ds(cut * ROWS_OF_CUT, ROWS_OF_CUT)], row_sem.at[4, cut])
+            came_in(3, 1, cut)
+            work_y(3, cut)
+            came_in(0, -1, cut)
             work_y(0, cut)
             work_y(1, cut)
+            work_y(2, cut)
             return_y(cut)
 
     for cut in range(3):
@@ -330,7 +356,7 @@
             total[x, y] += back_z[y, :, lanes_of(x)]
 
     for cut in range(CUTS):
-        arrived(back_y.at[:, pl.ds(cut * 2 * ROWS_OF_CUT, 2 * ROWS_OF_CUT)], row_sem.at[4, cut])
+        arrived(back_y.at[:, pl.ds(cut * 2 * ROWS_OF_CUT, 2 * ROWS_OF_CUT)], row_sem.at[5, cut])
         for upper in range(2):
 
             @pl.loop(0, ROWS_OF_CUT)
@@ -339,10 +365,10 @@
                 for x in range(8):
                     flat_total[pl.ds(x * 384 + z, 24, stride=16), :] += back_y[x, z]
 
-    arrived(u_stage.at[:, pl.ds(0, 14)], send_sem.at[0])
-    arrived(v_stage.at[:, pl.ds(0, 14)], send_sem.at[1])
-    arrived(back_y.at[:, pl.ds(0, 14)], send_sem.at[2])
-    arrived(back_y, send_sem.at[7])
+    arrived(u_stage.at[:, pl.ds(0, 12)], send_sem.at[0])
+    arrived(v_stage.at[:, pl.ds(0, 12)], send_sem.at[1])
+    arrived(back_y.at[:, pl.ds(0, 12)], send_sem.at[2])
+    arrived(u_y.at[pl.ds(0, 3)], send_sem.at[7])
     arrived(back_z.at[pl.ds(0, 21)], send_sem.at[3])
     arrived(back_z.at[pl.ds(0, 21)], send_sem.at[4])
     arrived(back_z, send_sem.at[5])
@@ -354,7 +380,7 @@
     field = pltpu.VMEM((24, 16, 1024), f32)
     tiled = pltpu.VMEM((8, 24, 16, 128), f32)
     staged = pltpu.VMEM((8, 16, 24, 128), f32)
-    half_y = pltpu.VMEM((2, 8, 192, 128), f32)
+    served_y = pltpu.VMEM((8, 384, 128), f32)
     half_z = pltpu.VMEM((3, 128, 1024), f32)
     result = pl.pallas_call(
         kernel,
@@ -365,11 +391,11 @@
             tiled, tiled, pltpu.VMEM((768, 1024), bf16),
             pltpu.VMEM((2, 1024, 1024), bf16), pltpu.VMEM((2, 384, 384), bf16),
             pltpu.VMEM((2, 4, 64, 256), bf16),
-            pltpu.VMEM((2, 384, 384), f32), pltpu.VMEM((2, 384, 384), bf16),
-            staged, staged, pltpu.VMEM((2, 8, 2, 192, 128), f32), half_y, half_y, staged,
+            pltpu.VMEM((2, 384, 384), f32), pltpu.VMEM((768, 384), bf16),
+            staged, staged, pltpu.VMEM((4, 8, 2, 192, 128), f32), served_y, served_y, staged,
             pltpu.VMEM((3, 4, 64, 1024), f32), half_z, half_z, field,
             pltpu.SemaphoreType.DMA((5,)), pltpu.SemaphoreType.DMA((8,)),
-            pltpu.SemaphoreType.DMA((7, CUTS)), pltpu.SemaphoreType.DMA((4, 3)),
+            pltpu.SemaphoreType.DMA((12, CUTS)), pltpu.SemaphoreType.DMA((4, 3)),
         ],
         compiler_params=pltpu.CompilerParams(
             collective_id=0, has_side_effects=True, vmem_limit_bytes=60 * 2**20

time: 107 us -> 103 us (0.963)
  Pallas kernels: 106 us -> 102 us
    pallas_call x1, Pallas kernels: 106 us -> 102 us  [shards(): pl.pallas_call(kernel, out_shape=pltpu.VMEM((8, 24, 16, 128), f32), in_sp...]
where the time goes in v2:
time: 103 us
  Pallas kernels  102 us (99%)
  local copies, waits for them, and re-layouts  1.35 us (1%)
    pallas_call x1, Pallas kernels, shards(): pl.pallas_call(kernel, out_shape=pltpu.VMEM((8, 24, 16, 128), f32), in_sp...  102 us

profile of v2, /device:TPU:1, one launch (start us, length us, event | category | flops | bytes accessed | tf_op | source)
XLA Modules:
  0.0 103.2 jit_solution(8423189132341180247)
XLA Ops:
  0.0 101.9 %momentum.1 = f32[8,24,16,128]{3,2,1,0:T(8,128)S(1)} custom-call(f32[24,16,1024]{2,1,0:T(8,128)} %u_hbm.1, f32[24,16,1024]{2,1,0:T(8,128)} %v_hbm.1, f32[24,16,1024]{2,1,0:T(8,128)} %w_hbm.1, bf16[2,1024,1024]{2,1,0:T(8,128)(2,1)} %mx_hbm.1, bf16[2,384,384]{2,1,0:T(8,128)(2,1)} %my_hbm.1, bf16[2,4,64,256]{3,2,1,0:T(8,128)(2,1)} %bitcast.7), custom_call_target="tpu_custom_call" | custom-call | flops 5000000000 | bytes 12582912 | tf_op jit(solution)/shard_map/momentum/pallas_call | solution.py:385
  101.9 1.3 %copy_bitcast_fusion = f32[24,16,1024]{2,1,0:T(8,128)} fusion(f32[8,24,16,128]{3,2,1,0:T(8,128)S(1)} %momentum.1), kind=kLoop, calls=%fused_computation | loop fusion | bytes 3145728 | tf_op jit(solution)/shard_map/reshape | solution.py:406

commit v3 on v2

--- a/solution.py
+++ b/solution.py
@@ -9,8 +9,9 @@
 
 viscosity = 0.5
 MESH = pl.DeviceIdType.MESH
-CUTS = 4
-ROWS_OF_CUT = 8 // CUTS
+CUT_ROWS = (2, 2, 2, 2)
+CUT_AT = (0, 2, 4, 6)
+CUTS = len(CUT_ROWS)
 BASE = (0, 288, 336, 144)
 SERVED = (144, 48, 48, 144)
 ROUTES = ((0, 2), (3, 2), (0, 1), (3, 1), (0, 0), (3, 0), (1, 0), (2, 0))
@@ -57,11 +58,6 @@
     def lanes_of(x):
         return slice(x * 128, (x + 1) * 128)
 
-    for x in range(8):
-        pltpu.make_async_copy(u_hbm.at[:, :, lanes_of(x)], u_own.at[x], load_sem.at[0]).start()
-    for x in range(8):
-        pltpu.make_async_copy(v_hbm.at[:, :, lanes_of(x)], v_own.at[x], load_sem.at[1]).start()
-
     barrier = pltpu.get_barrier_semaphore()
 
     def greet(x, z):
@@ -79,9 +75,9 @@
         )
 
     pl.semaphore_signal(barrier, inc=1, device_id=(row, partner), device_id_type=MESH)
-    pltpu.make_async_copy(mx_hbm, mat_x, load_sem.at[2]).start()
-    pltpu.make_async_copy(my_hbm, mat_y, load_sem.at[3]).start()
-    pltpu.make_async_copy(mz_hbm, mat_z, load_sem.at[4]).start()
+
+    for x in range(8):
+        pltpu.make_async_copy(u_hbm.at[:, :, lanes_of(x)], u_own.at[x], load_sem.at[0]).start()
 
     def arrived(ref, sem):
         pltpu.make_async_copy(ref, ref, sem).wait()
@@ -90,9 +86,9 @@
         flat = own.reshape(8 * 24 * 16, 128)
         for upper in range(2):
 
-            @pl.loop(0, ROWS_OF_CUT)
+            @pl.loop(0, CUT_ROWS[cut])
             def _(step):
-                z = upper * 8 + cut * ROWS_OF_CUT + step
+                z = upper * 8 + CUT_AT[cut] + step
                 for x in range(8):
                     stage[x, z] = flat[pl.ds(x * 384 + z, 24, stride=16), :]
 
@@ -100,9 +96,11 @@
         served = 2 - j if role == 0 else j
         return pl.ds(pl.multiple_of(BASE[role] + served * 48 + x * 24, 8), 24)
 
-    def over_row(piece, kind, cut, sems):
-        for role, j in ROUTES:
-            for x in (1 - x_me, x_me):
+    def over_row(piece, kind, cut, sems, roles=(0, 1, 2, 3)):
+        for x in (1 - x_me, x_me):
+            for role, j in ROUTES:
+                if role not in roles:
+                    continue
                 src, dst, to = piece(x, j, role)
                 if j == 0 and x is x_me:
                     pltpu.make_async_copy(src, dst, sems(role)).start()
@@ -113,12 +111,12 @@
                     ).start()
 
     def send_row(stage, pencil, kind, cut):
-        rows = pl.ds(cut * ROWS_OF_CUT, ROWS_OF_CUT)
+        rows = pl.ds(CUT_AT[cut], CUT_ROWS[cut])
 
         def piece(x, j, role):
             to = around(z_me + j) if role == 0 else around(z_me - j)
             group = around(to - role)
-            src = stage.at[group, pl.ds(x * 8 + cut * ROWS_OF_CUT, ROWS_OF_CUT)]
+            src = stage.at[group, pl.ds(x * 8 + CUT_AT[cut], CUT_ROWS[cut])]
             if kind == 0:
                 dst = pencil.at[role, rows, x_me, pl.ds(pl.multiple_of(z_me * 24, 8), 24), :]
             else:
@@ -133,7 +131,7 @@
     def pass_on(role, step, cut):
         to = row_of(x_me, z_me + step)
         first = z_me - role - 2 if step == 1 else z_me
-        rows = pl.ds(cut * ROWS_OF_CUT, ROWS_OF_CUT)
+        rows = pl.ds(CUT_AT[cut], CUT_ROWS[cut])
 
         @pl.loop(0, 3 + role if step == 1 else 6 - role)
         def _(i):
@@ -150,13 +148,13 @@
     def came_in(role, step, cut):
         count = 2 + role if step == 1 else 5 - role
         arrived(
-            v_y.at[pl.ds(cut * ROWS_OF_CUT, ROWS_OF_CUT), pl.ds(0, 48 * count)],
+            v_y.at[pl.ds(CUT_AT[cut], CUT_ROWS[cut]), pl.ds(0, 48 * count)],
             row_sem.at[(5 if step == 1 else 9) + role, cut],
         )
 
     def own_part(role, cut):
         arrived(
-            v_y.at[pl.ds(cut * ROWS_OF_CUT, ROWS_OF_CUT), pl.ds(BASE[role], SERVED[role])],
+            v_y.at[pl.ds(CUT_AT[cut], CUT_ROWS[cut]), pl.ds(BASE[role], SERVED[role])],
             row_sem.at[role, cut],
         )
 
@@ -185,6 +183,8 @@
             pltpu.make_async_copy(src, dst, col_sem.at[kind, cut]).start()
 
     arrived(u_own, load_sem.at[0])
+    for x in range(8):
+        pltpu.make_async_copy(v_hbm.at[:, :, lanes_of(x)], v_own.at[x], load_sem.at[1]).start()
     restage(u_own, u_stage, 0)
     pl.semaphore_wait(barrier, 17)
     send_row(u_stage, u_y, 0, 0)
@@ -192,6 +192,9 @@
     for cut in range(1, CUTS):
         restage(u_own, u_stage, cut)
         send_row(u_stage, u_y, 0, cut)
+    pltpu.make_async_copy(mx_hbm, mat_x, load_sem.at[2]).start()
+    pltpu.make_async_copy(my_hbm, mat_y, load_sem.at[3]).start()
+    pltpu.make_async_copy(mz_hbm, mat_z, load_sem.at[4]).start()
     arrived(v_own, load_sem.at[1])
     for cut in range(CUTS):
         restage(v_own, v_stage, cut)
@@ -254,36 +257,34 @@
     def work_y(role, cut):
         base, count = BASE[role], SERVED[role]
 
-        @pl.loop(0, ROWS_OF_CUT // 2)
-        def _(pair):
-            z = cut * ROWS_OF_CUT + pair * 2
-            both = product(
-                lhs_y[2 * base : 2 * (base + count), :],
-                jnp.concatenate(
-                    [u_y[role, z + i].reshape(384, 128) for i in range(2)], axis=1
-                ),
+        at, wide = CUT_AT[cut], CUT_ROWS[cut]
+        both = product(
+            lhs_y[2 * base : 2 * (base + count), :],
+            jnp.concatenate(
+                [u_y[role, at + i].reshape(384, 128) for i in range(wide)], axis=1
+            ),
+        )
+        for i in range(wide):
+            lanes = lanes_of(i)
+            term_y[at + i, base : base + count] = (
+                -v_y[at + i, base : base + count] * both[:count, lanes]
+                + viscosity * both[count:, lanes]
             )
-            for i in range(2):
-                lanes = lanes_of(i)
-                term_y[z + i, base : base + count] = (
-                    -v_y[z + i, base : base + count] * both[:count, lanes]
-                    + viscosity * both[count:, lanes]
-                )
-
-    def return_y(cut):
-        rows = pl.ds(cut * ROWS_OF_CUT, ROWS_OF_CUT)
+
+    def return_y(cut, roles):
+        rows = pl.ds(CUT_AT[cut], CUT_ROWS[cut])
 
         def piece(x, j, role):
             to = around(z_me - j) if role == 0 else around(z_me + j)
             return (
                 term_y.at[rows, slot(role, j, x), :],
                 back_y.at[
-                    around(z_me - role), pl.ds(x_me * 8 + cut * ROWS_OF_CUT, ROWS_OF_CUT)
+                    around(z_me - role), pl.ds(x_me * 8 + CUT_AT[cut], CUT_ROWS[cut])
                 ],
                 x * 8 + to,
             )
 
-        over_row(piece, 2, cut, lambda role: row_sem.at[5, cut])
+        over_row(piece, 2, cut, lambda role: row_sem.at[5, cut], roles)
 
     def work_z(cut):
         arrived(u_z.at[cut, :, other_half, :], col_sem.at[3, cut])
@@ -338,14 +339,16 @@
         if cut < 3:
             work_z(cut)
         if cut < CUTS:
-            arrived(v_y.at[pl.ds(cut * ROWS_OF_CUT, ROWS_OF_CUT)], row_sem.at[4, cut])
+            arrived(v_y.at[pl.ds(CUT_AT[cut], CUT_ROWS[cut])], row_sem.at[4, cut])
+            work_y(1, cut)
+            work_y(2, cut)
+            return_y(cut, (1, 2))
             came_in(3, 1, cut)
             work_y(3, cut)
+            return_y(cut, (3,))
             came_in(0, -1, cut)
             work_y(0, cut)
-            work_y(1, cut)
-            work_y(2, cut)
-            return_y(cut)
+            return_y(cut, (0,))
 
     for cut in range(3):
         arrived(back_z.at[pl.ds(cut * 8, 8)], col_sem.at[2, cut])
@@ -356,12 +359,12 @@
             total[x, y] += back_z[y, :, lanes_of(x)]
 
     for cut in range(CUTS):
-        arrived(back_y.at[:, pl.ds(cut * 2 * ROWS_OF_CUT, 2 * ROWS_OF_CUT)], row_sem.at[5, cut])
+        arrived(back_y.at[:, pl.ds(0, 2 * CUT_ROWS[cut])], row_sem.at[5, cut])
         for upper in range(2):
 
-            @pl.loop(0, ROWS_OF_CUT)
+            @pl.loop(0, CUT_ROWS[cut])
             def _(step):
-                z = upper * 8 + cut * ROWS_OF_CUT + step
+                z = upper * 8 + CUT_AT[cut] + step
                 for x in range(8):
                     flat_total[pl.ds(x * 384 + z, 24, stride=16), :] += back_y[x, z]
 

time: 103 us -> 102 us (level)
  Pallas kernels: 102 us -> 100 us
    pallas_call x1, Pallas kernels: 102 us -> 100 us  [shards(): pl.pallas_call(kernel, out_shape=pltpu.VMEM((8, 24, 16, 128), f32), in_sp...]
where the time goes in v3:
time: 102 us
  Pallas kernels  100 us (98%)
  local copies, waits for them, and re-layouts  1.35 us (1%)
    pallas_call x1, Pallas kernels, shards(): pl.pallas_call(kernel, out_shape=pltpu.VMEM((8, 24, 16, 128), f32), in_sp...  100 us

profile of v3, /device:TPU:1, one launch (start us, length us, event | category | flops | bytes accessed | tf_op | source)
XLA Modules:
  0.0 101.8 jit_solution(14266372347014734409)
XLA Ops:
  0.0 100.5 %momentum.1 = f32[8,24,16,128]{3,2,1,0:T(8,128)S(1)} custom-call(f32[24,16,1024]{2,1,0:T(8,128)} %u_hbm.1, f32[24,16,1024]{2,1,0:T(8,128)} %v_hbm.1, f32[24,16,1024]{2,1,0:T(8,128)} %w_hbm.1, bf16[2,1024,1024]{2,1,0:T(8,128)(2,1)} %mx_hbm.1, bf16[2,384,384]{2,1,0:T(8,128)(2,1)} %my_hbm.1, bf16[2,4,64,256]{3,2,1,0:T(8,128)(2,1)} %bitcast.7), custom_call_target="tpu_custom_call" | custom-call | flops 5000000000 | bytes 12582912 | tf_op jit(solution)/shard_map/momentum/pallas_call | solution.py:388
  100.5 1.3 %copy_bitcast_fusion = f32[24,16,1024]{2,1,0:T(8,128)} fusion(f32[8,24,16,128]{3,2,1,0:T(8,128)S(1)} %momentum.1), kind=kLoop, calls=%fused_computation | loop fusion | bytes 3145728 | tf_op jit(solution)/shard_map/reshape | solution.py:409

commit v4 on v3

--- a/solution.py
+++ b/solution.py
@@ -96,13 +96,14 @@
         served = 2 - j if role == 0 else j
         return pl.ds(pl.multiple_of(BASE[role] + served * 48 + x * 24, 8), 24)
 
-    def over_row(piece, kind, cut, sems, roles=(0, 1, 2, 3)):
-        for x in (1 - x_me, x_me):
+    def over_row(piece, kind, cut, sems, roles=(0, 1, 2, 3), sides=(1, 0)):
+        for side in sides:
+            x = 1 - x_me if side else x_me
             for role, j in ROUTES:
                 if role not in roles:
                     continue
                 src, dst, to = piece(x, j, role)
-                if j == 0 and x is x_me:
+                if j == 0 and not side:
                     pltpu.make_async_copy(src, dst, sems(role)).start()
                 else:
                     pltpu.make_async_remote_copy(
@@ -110,7 +111,7 @@
                         recv_sem=sems(role), device_id=(to, col), device_id_type=MESH,
                     ).start()
 
-    def send_row(stage, pencil, kind, cut):
+    def send_row(stage, pencil, kind, cut, sides=(1, 0)):
         rows = pl.ds(CUT_AT[cut], CUT_ROWS[cut])
 
         def piece(x, j, role):
@@ -126,6 +127,7 @@
         over_row(
             piece, kind, cut,
             lambda role: row_sem.at[role, cut] if kind == 0 else row_sem.at[4, cut],
+            sides=sides,
         )
 
     def pass_on(role, step, cut):
@@ -198,7 +200,9 @@
     arrived(v_own, load_sem.at[1])
     for cut in range(CUTS):
         restage(v_own, v_stage, cut)
-        send_row(v_stage, v_y, 1, cut)
+        send_row(v_stage, v_y, 1, cut, (1,))
+    for cut in range(CUTS):
+        send_row(v_stage, v_y, 1, cut, (0,))
     send_col(w_hbm, w_z, 1)
 
     flat_total = total.reshape(8 * 24 * 16, 128)

time: 102 us -> 102 us (level)
  no operation moved by 1% of the time
where the time goes in v4:
time: 102 us
  Pallas kernels  101 us (99%)
  local copies, waits for them, and re-layouts  1.35 us (1%)
    pallas_call x1, Pallas kernels, shards(): pl.pallas_call(kernel, out_shape=pltpu.VMEM((8, 24, 16, 128), f32), in_sp...  101 us

profile of v4, /device:TPU:1, one launch (start us, length us, event | category | flops | bytes accessed | tf_op | source)
XLA Modules:
  0.0 101.9 jit_solution(17036582366516630380)
XLA Ops:
  0.0 100.5 %momentum.1 = f32[8,24,16,128]{3,2,1,0:T(8,128)S(1)} custom-call(f32[24,16,1024]{2,1,0:T(8,128)} %u_hbm.1, f32[24,16,1024]{2,1,0:T(8,128)} %v_hbm.1, f32[24,16,1024]{2,1,0:T(8,128)} %w_hbm.1, bf16[2,1024,1024]{2,1,0:T(8,128)(2,1)} %mx_hbm.1, bf16[2,384,384]{2,1,0:T(8,128)(2,1)} %my_hbm.1, bf16[2,4,64,256]{3,2,1,0:T(8,128)(2,1)} %bitcast.7), custom_call_target="tpu_custom_call" | custom-call | flops 5000000000 | bytes 12582912 | tf_op jit(solution)/shard_map/momentum/pallas_call | solution.py:392
  100.5 1.3 %copy_bitcast_fusion = f32[24,16,1024]{2,1,0:T(8,128)} fusion(f32[8,24,16,128]{3,2,1,0:T(8,128)S(1)} %momentum.1), kind=kLoop, calls=%fused_computation | loop fusion | bytes 3145728 | tf_op jit(solution)/shard_map/reshape | solution.py:413
